TPU v7x, 32 devices: a whole 2x2x4 slice. The times are simulated.
32 devices in a mesh: dp: 16 (over z, y, core), mp: 2 (over x).
Axes of the slice: x: 2, y: 2, z: 4, core: 2. Of those that a mesh axis runs over, the one named last changes fastest.
Arguments:
- embed_in: bfloat16 [4096, 6144], P('dp', 'mp'), may hold values from -7.5 to 7.5
- block_grad: bfloat16 [4096, 6144], P('dp', 'mp'), may hold values from -6 to 6
- attn_grad: bfloat16 [4096, 6144], P('dp', 'mp'), may hold values from -5.7 to 5.7
- hidden_grad: bfloat16 [4096, 12288], P('dp', 'mp'), may hold values from -6 to 6
- up_weight: bfloat16 [6144, 12288], P('dp', 'mp'), may hold values from -0.078125 to 0.078125
- up_bias: float32 [12288], P('mp'), may hold values from -4 to 4
- norm_gain: float32 [6144], P('mp'), may hold values from 0.1 to 1.9
- patches: bfloat16 [4096, 588], P('dp'), may hold values from -5 to 5
Outputs:
- embed_grad: bfloat16 [4096, 6144], P('dp', 'mp')
- patch_weight_grad: float32 [588, 6144], P(None, 'mp')
All inputs are finite; a program needn't handle non-finite values.
Results may differ from a plain program's by a relative error of at most 0.0046.
Values may be sent and summed in bfloat16 or wider, within the bound.
A program may use at most 192 MiB of HBM per device.

v0:
```python
import jax
import jax.numpy as jnp
from jax import lax
from jax.sharding import PartitionSpec as P

D = 6144
IMAGES = 1


def gelu_slope(values):
    cdf_part = 0.5 * (1.0 + jax.scipy.special.erf(values * 0.7071067811865476))
    density = jnp.exp(-0.5 * values * values) * 0.3989422804014327
    return cdf_part + values * density


def body(embed_in, block_grad, attn_grad, hidden_grad, up_weight, up_bias, norm_gain, patches):
    features = embed_in.astype(jnp.float32)
    row_total, row_square = lax.psum(
        (
            jnp.sum(features, axis=-1, keepdims=True),
            jnp.sum(features * features, axis=-1, keepdims=True),
        ),
        "mp",
    )
    row_mean = row_total / D
    centred = features - row_mean
    variance = jnp.maximum(row_square / D - row_mean * row_mean, 0.0)
    inv_std = lax.rsqrt(variance + 1e-06)
    unit = centred * inv_std
    normed = (unit * norm_gain).astype(jnp.bfloat16)
    weights = lax.all_gather(up_weight, "dp", axis=0, tiled=True)
    preact = (
        jnp.dot(
            lax.all_gather(normed, "mp", axis=1, tiled=True),
            weights,
            preferred_element_type=jnp.float32,
        )
        + up_bias
    )
    delta = (hidden_grad.astype(jnp.float32) * gelu_slope(preact)).astype(jnp.bfloat16)
    terms = lax.dot_general(
        delta, weights, (((1,), (1,)), ((), ())), preferred_element_type=jnp.float32
    )
    columns = embed_in.shape[1]
    full_sum = lax.psum(terms, "mp")
    own_sum = lax.dynamic_slice_in_dim(full_sum, lax.axis_index("mp") * columns, columns, 1)
    branch = own_sum + attn_grad.astype(jnp.float32)
    scaled = branch * norm_gain
    scaled_total, paired_total = lax.psum(
        (jnp.sum(scaled, axis=-1, keepdims=True), jnp.sum(scaled * unit, axis=-1, keepdims=True)),
        "mp",
    )
    norm_back = inv_std * (scaled - scaled_total / D - unit * (paired_total / D))
    embed_grad = (block_grad.astype(jnp.float32) + norm_back).astype(jnp.bfloat16)
    factor = 1.0 / (lax.axis_size("dp") * IMAGES)
    partial_grad = (
        lax.dot_general(
            patches, embed_grad, (((0,), (0,)), ((), ())), preferred_element_type=jnp.float32
        )
        * factor
    )
    patch_weight_grad = lax.psum(partial_grad, "dp")
    return (embed_grad, patch_weight_grad)


def solution(mesh):
    in_specs = (
        P("dp", "mp"),
        P("dp", "mp"),
        P("dp", "mp"),
        P("dp", "mp"),
        P("dp", "mp"),
        P("mp"),
        P("mp"),
        P("dp", None),
    )
    out_specs = (P("dp", "mp"), P(None, "mp"))
    return jax.shard_map(body, mesh=mesh, in_specs=in_specs, out_specs=out_specs, check_vma=False)
```

profile of v0, /device:TPU:0, one launch (start us, length us, event | category | flops | bytes accessed | tf_op | source)
XLA Modules:
  0.0 833.0 jit_solution(18403482228381995495)
XLA Ops:
  7.2 0.0 copy-start
  7.2 0.0 all-gather.3.cloned.1.call-start
  7.2 2.0 fusion.8
  9.2 5.8 all-reduce.1
  15.0 3.2 fusion.13
  18.3 0.0 copy-start.5
  18.3 0.0 copy-start.6
  18.3 0.0 all-gather.3.cloned.1.call-update
  18.3 0.0 all-gather.5.cloned.1.call-start
  18.3 0.7 all-gather.5.cloned.1.call-update
  19.0 0.0 all-reduce.5.cloned.1.call-start
  19.1 46.1 %all-gather.3.cloned.1.call-done = bf16[256,6144]{1,0:T(8,128)(2,1)} async-done(((bf16[256,3072]{1,0:T(8,128)(2,1)}), bf16[256,6144]{1,0:T(8,128)(2,1)}) %all-gather.3.cloned.1.call-update) | async-done | bytes 3145744 | tf_op jit(solution)/shard_map/all_gather | solution.py:34
  65.2 367.3 %all-gather.5.cloned.1.call-done = bf16[6144,6144]{1,0:T(8,128)(2,1)} async-done(((bf16[384,6144]{1,0:T(8,128)(2,1)}), bf16[6144,6144]{1,0:T(8,128)(2,1)}) %all-gather.5.cloned.1.call-update) | async-done | bytes 75497488 | tf_op jit(solution)/shard_map/all_gather | solution.py:31
  432.4 0.0 copy-done.5
  432.4 0.0 copy-done.6
  432.4 31.8 %fusion.5.clone.4 = bf16[256,6144]{1,0:T(8,128)(2,1)} fusion(bf16[256,6144]{1,0:T(8,128)(2,1)} %all-gather.3.cloned.1.call-done, bf16[6144,6144]{1,0:T(8,128)(2,1)} %all-gather.5.cloned.1.call-done, bf16[256,6144]{1,0:T(8,128)(2,1)S(1)} %copy-done.5, f32[6144]{0:T(1024)S(1)} %copy-done.6), kind=kOutput, calls=%fused_computation.8.clone.clone.clone.1 | convolution fusion | flops 19346227200 | bytes 84959232 | tf_op jit(solution)/shard_map/dot_general | solution.py:33
  464.2 31.4 %fusion.6 = f32[256,6144]{1,0:T(8,128)} fusion(bf16[6144,6144]{1,0:T(8,128)(2,1)} %all-gather.5.cloned.1.call-done, bf16[256,6144]{1,0:T(8,128)(2,1)} %fusion.5.clone.4), kind=kOutput, calls=%fused_computation.9 | convolution fusion | flops 19327352832 | bytes 84934656 | tf_op jit(solution)/shard_map/dot_general | solution.py:41
  495.6 0.0 copy-start.1
  495.6 0.0 copy-start.3
  495.6 0.0 copy-start.4
  495.6 0.0 all-reduce.5.cloned.1.call-update
  495.6 0.0 all-reduce.7.cloned.1.call-start
  495.7 153.3 %all-reduce.5.cloned.1.call-done = f32[256,6144]{1,0:T(8,128)} async-done(((f32[256,6144]{1,0:T(8,128)}), f32[256,6144]{1,0:T(8,128)}) %all-reduce.5.cloned.1.call-update) | async-done | bytes 6291472 | tf_op jit(solution)/shard_map/psum | solution.py:45
  649.0 0.0 copy-done.1
  649.0 0.0 copy-done.3
  649.0 0.0 copy-done.4
  649.0 3.0 fusion.25
  652.0 5.1 all-reduce
  657.1 4.7 fusion.18
  661.9 0.0 copy-done
  661.9 0.0 copy-start.2
  661.9 4.2 multiply_bitcast_fusion
  666.1 0.0 copy-done.2
  666.1 0.0 all-reduce.7.cloned.1.call-update
  666.1 153.4 %all-reduce.7.cloned.1.call-done = f32[588,3072]{1,0:T(8,128)} async-done(((f32[588,3072]{1,0:T(8,128)}), f32[588,3072]{1,0:T(8,128)}) %all-reduce.7.cloned.1.call-update) | async-done | bytes 7225360 | tf_op jit(solution)/shard_map/psum | solution.py:62
  819.5 7.0 copy.12
  (2 shorter events, 0.0 us)
Async XLA Ops:
  7.2 654.7 %copy-start = (bf16[256,588]{0,1:T(8,128)(2,1)S(1)}, bf16[256,588]{0,1:T(8,128)(2,1)}, u32[]{:S(2)}) copy-start(bf16[256,588]{0,1:T(8,128)(2,1)} %param.15) | copy-start | bytes 903172
  7.2 58.0 %all-gather.3.cloned.1.call-start = ((), (), s32[]{:S(2)}) async-start(), calls=%async_computation | async-start | bytes 4718592 | tf_op jit(solution)/shard_map/all_gather | solution.py:34
  18.3 414.2 %copy-start.5 = (bf16[256,6144]{1,0:T(8,128)(2,1)S(1)}, bf16[256,6144]{1,0:T(8,128)(2,1)}, u32[]{:S(2)}) copy-start(bf16[256,6144]{1,0:T(8,128)(2,1)} %param.11) | copy-start | bytes 9437188
  18.3 414.2 %copy-start.6 = (f32[6144]{0:T(1024)S(1)}, f32[6144]{0:T(1024)}, u32[]{:S(2)}) copy-start(f32[6144]{0:T(1024)} %param.13) | copy-start | bytes 73732
  18.3 414.1 %all-gather.5.cloned.1.call-start = ((), (), s32[]{:S(2)}) async-start(), calls=%async_computation.1 | async-start | bytes 80216064 | tf_op jit(solution)/shard_map/all_gather | solution.py:31
  19.0 629.9 %all-reduce.5.cloned.1.call-start = ((), (), s32[]{:S(2)}) async-start(), calls=%async_computation.2 | async-start | bytes 12582912 | tf_op jit(solution)/shard_map/psum | solution.py:45
  495.6 153.4 %copy-start.1 = (bf16[256,3072]{1,0:T(8,128)(2,1)S(1)}, bf16[256,3072]{1,0:T(8,128)(2,1)}, u32[]{:S(2)}) copy-start(bf16[256,3072]{1,0:T(8,128)(2,1)} %param.8) | copy-start | bytes 4718596
  495.6 153.4 %copy-start.3 = (bf16[256,3072]{1,0:T(8,128)(2,1)S(1)}, bf16[256,3072]{1,0:T(8,128)(2,1)}, u32[]{:S(2)}) copy-start(bf16[256,3072]{1,0:T(8,128)(2,1)} %param.10) | copy-start | bytes 4718596
  495.6 153.4 %copy-start.4 = (f32[3072]{0:T(1024)S(1)}, f32[3072]{0:T(1024)}, u32[]{:S(2)}) copy-start(f32[3072]{0:T(1024)} %param.14) | copy-start | bytes 36868
  495.6 323.9 %all-reduce.7.cloned.1.call-start = ((), (), s32[]{:S(2)}) async-start(), calls=%async_computation.3 | async-start | bytes 14548992 | tf_op jit(solution)/shard_map/psum | solution.py:62
  661.9 4.2 copy-start.2
Sparse Core Ops, SparseCore 0:
  18.4 46.7 all-gather.2
  66.8 365.6 all-gather.4
  495.8 153.1 all-reduce.4
  666.2 153.2 all-reduce.6
where the time goes:
time: 833 us
  waiting for transfers between devices  721 us (87%)
  matrix products  67.3 us (8%)
  between operations  13.8 us (2%)
  other arithmetic  13 us (2%)
  blocking collectives  11 us (1%)
    all_gather x1, waiting for transfers between devices, body(): weights = lax.all_gather(up_weight, 'dp', axis=0, tiled=True)  367 us
    psum x1, waiting for transfers between devices, body(): patch_weight_grad = lax.psum(partial_grad, 'dp')  153 us
    psum x1, waiting for transfers between devices, body(): full_sum = lax.psum(terms, 'mp')  153 us
    all_gather x1, waiting for transfers between devices, body(): lax.all_gather(normed, 'mp', axis=1, tiled=True)  46.1 us
    dot_general x1, matrix products, body(): jnp.dot(lax.all_gather(normed, 'mp', axis=1, tiled=True), weights, prefer...  31.8 us
    dot_general x1, matrix products, body(): lax.dot_general(delta, weights, (((1,), (1,)), ((), ())), preferred_eleme...  31.4 us
  transfers between devices with their start and end apart: 4, of which 4 were waited for; matrix products, arithmetic and copies ran while one was open for 0% of the time, Pallas kernels for 0%

commit v1 on v0

v1 whole, which is shorter than its diff:
```python
import math

import jax
import jax.numpy as jnp
from jax import lax
from jax.experimental import pallas as pl
from jax.sharding import PartitionSpec as P

D = 6144
IMAGES = 1
PIECES = 2


def gelu_slope(values):
    cdf_part = 0.5 * (1.0 + lax.erf(values * 0.7071067811865476))
    density = jnp.exp(-0.5 * values * values) * 0.3989422804014327
    return cdf_part + values * density


def swap(value):
    return lax.ppermute(value, "mp", [(0, 1), (1, 0)])


def gather_features(value, groups):
    if groups != 2:
        return lax.all_gather(value, "mp", axis=value.ndim - 1, tiled=True)
    other = swap(value)
    first = lax.axis_index("mp") == 0
    return jnp.concatenate([jnp.where(first, value, other), jnp.where(first, other, value)], -1)


def spread(part, name):
    count, width, rows = part.shape
    group = 128 // math.gcd(width, 128)

    def kernel(blocks_ref, out_ref):
        blocks = blocks_ref[...].astype(jnp.float32).reshape(group * width, rows)
        out_ref[...] = blocks.T

    return pl.pallas_call(
        kernel,
        grid=(count // group,),
        in_specs=[pl.BlockSpec((group, width, rows), lambda i: (i, 0, 0))],
        out_specs=pl.BlockSpec((rows, group * width), lambda i: (0, i)),
        out_shape=jax.ShapeDtypeStruct((rows, count * width), jnp.float32),
        name=name,
    )(part)


def tokens_product(left, right):
    return lax.dot_general(
        left, right, (((0,), (0,)), ((), ())), preferred_element_type=jnp.float32
    )


def patch_grad(patches_all, embed_grad):
    n = lax.axis_size("dp")
    factor = 1.0 / (n * IMAGES)
    columns = embed_grad.shape[1] // n
    mine = embed_grad.reshape(-1, n, columns).transpose(1, 0, 2)
    mine = lax.all_to_all(mine, "dp", 0, 0)
    part = tokens_product(mine.reshape(-1, columns), patches_all) * factor
    return spread(lax.all_gather(part.astype(jnp.bfloat16), "dp", axis=0), "spread_columns")


def branch_sum(delta, weight, normed, gain_all, groups):
    transposed = (((1,), (1,)), ((), ()))
    if groups != 2:
        terms = lax.dot_general(delta, weight, transposed, preferred_element_type=jnp.float32)
        own = lax.psum_scatter(terms, "mp", scatter_dimension=1, tiled=True)
        scaled = (terms * gain_all).sum(-1, keepdims=True)
        return own, scaled, (terms * normed.astype(jnp.float32)).sum(-1, keepdims=True)
    half = weight.shape[0] // 2
    width = half // PIECES
    first = lax.axis_index("mp") == 0
    own, scaled, paired = [], 0.0, 0.0
    for piece in range(PIECES):
        sides = []
        for start in (piece * width, half + piece * width):
            rows = slice(start, start + width)
            term = lax.dot_general(
                delta, weight[rows], transposed, preferred_element_type=jnp.float32
            )
            scaled += (term * gain_all[rows]).sum(-1, keepdims=True)
            paired += (term * normed[:, rows].astype(jnp.float32)).sum(-1, keepdims=True)
            sides.append(term)
        arrived = swap(jnp.where(first, sides[1], sides[0]).astype(jnp.bfloat16))
        own.append(jnp.where(first, sides[0], sides[1]) + arrived.astype(jnp.float32))
    return jnp.concatenate(own, axis=1), scaled, paired


def body(embed_in, block_grad, attn_grad, hidden_grad, up_weight, up_bias, norm_gain, patches):
    groups = lax.axis_size("mp")
    weight = lax.all_gather(up_weight, "dp", axis=0, tiled=True)
    patches_all = lax.all_gather(patches, "dp", axis=0, tiled=True)
    gain_all = gather_features(norm_gain, groups)
    features = embed_in.astype(jnp.float32)
    row_total, row_square = lax.psum(
        (
            jnp.sum(features, axis=-1, keepdims=True),
            jnp.sum(features * features, axis=-1, keepdims=True),
        ),
        "mp",
    )
    row_mean = row_total / D
    centred = features - row_mean
    variance = jnp.maximum(row_square / D - row_mean * row_mean, 0.0)
    inv_std = lax.rsqrt(variance + 1e-06)
    unit = centred * inv_std
    normed = gather_features((unit * norm_gain).astype(jnp.bfloat16), groups)
    normed, gain_all = lax.optimization_barrier((normed, gain_all))
    preact = jnp.dot(normed, weight, preferred_element_type=jnp.float32) + up_bias
    delta = (hidden_grad.astype(jnp.float32) * gelu_slope(preact)).astype(jnp.bfloat16)
    own_sum, scaled_share, paired_share = branch_sum(delta, weight, normed, gain_all, groups)
    attn = attn_grad.astype(jnp.float32)
    attn_scaled = attn * norm_gain
    scaled_total, paired_total = lax.psum(
        (
            scaled_share + jnp.sum(attn_scaled, axis=-1, keepdims=True),
            paired_share + jnp.sum(attn_scaled * unit, axis=-1, keepdims=True),
        ),
        "mp",
    )
    scaled = (own_sum + attn) * norm_gain
    norm_back = inv_std * (scaled - scaled_total / D - unit * (paired_total / D))
    embed_grad = (block_grad.astype(jnp.float32) + norm_back).astype(jnp.bfloat16)
    return (embed_grad, patch_grad(patches_all, embed_grad))


def solution(mesh):
    in_specs = (
        P("dp", "mp"),
        P("dp", "mp"),
        P("dp", "mp"),
        P("dp", "mp"),
        P("dp", "mp"),
        P("mp"),
        P("mp"),
        P("dp", None),
    )
    out_specs = (P("dp", "mp"), P(None, "mp"))
    return jax.shard_map(body, mesh=mesh, in_specs=in_specs, out_specs=out_specs, check_vma=False)
```

time: 833 us -> 599 us (0.72)
  waiting for transfers between devices: 721 us -> 423 us
  blocking collectives: 11 us -> 51.4 us
  matrix products: 67.3 us -> 80.9 us
    psum x2 -> x0, waiting for transfers between devices: 307 us -> none  [the longest x1 153 us: body(): patch_weight_grad = lax.psum(partial_grad, 'dp')]
    ppermute x0 -> x4, waiting for transfers between devices: none -> 52.4 us  [swap(): return lax.ppermute(value, 'mp', [(0, 1), (1, 0)])]
    all_gather x2 -> x3, waiting for transfers between devices: 413 us -> 369 us  [the longest x1 321 us: body(): weight = lax.all_gather(up_weight, 'dp', axis=0, tiled=True)]
    all_to_all x0 -> x1, blocking collectives: none -> 40.6 us  [patch_grad(): mine = lax.all_to_all(mine, 'dp', 0, 0)]
    dot_general x3 -> x6, matrix products: 67.3 us -> 80.9 us  [the longest x4 43.4 us: branch_sum(): lax.dot_general(delta, weight[rows], transposed, preferred_element_type=j...]
  transfers between devices with their start and end apart: 4 -> 7, of which waited for: 4 -> 4; matrix products, arithmetic and copies ran while one was open for 0% -> 16% of each run, Pallas kernels for 0% -> 0%
where the time goes in v1:
time: 599 us; the launch traced here: 598 us
  waiting for transfers between devices  423 us (71%)
  matrix products  80.9 us (14%)
  blocking collectives  51.4 us (9%)
  other arithmetic  15.3 us (3%)
  between operations  13.9 us (2%)
  Pallas kernels  7.55 us (1%)
    all_gather x1, waiting for transfers between devices, body(): weight = lax.all_gather(up_weight, 'dp', axis=0, tiled=True)  321 us
    ppermute x4, waiting for transfers between devices, swap(): return lax.ppermute(value, 'mp', [(0, 1), (1, 0)])  52.4 us
    all_gather x1, waiting for transfers between devices, patch_grad(): lax.all_gather(part.astype(jnp.bfloat16), 'dp', axis=0)  48.4 us
    dot_general x4, matrix products, branch_sum(): lax.dot_general(delta, weight[rows], transposed, preferred_element_type=j...  43.4 us
    all_to_all x1, blocking collectives, patch_grad(): mine = lax.all_to_all(mine, 'dp', 0, 0)  40.6 us
    dot_general x1, matrix products, body(): jnp.dot(normed, weight, preferred_element_type=jnp.float32) + up_bias  32.6 us
  transfers between devices with their start and end apart: 7, of which 4 were waited for; matrix products, arithmetic and copies ran while one was open for 16% of the time, Pallas kernels for 0%

profile of v1, /device:TPU:0, one launch (start us, length us, event | category | flops | bytes accessed | tf_op | source)
XLA Modules:
  0.0 598.2 jit_solution(13049595038641396884)
XLA Ops:
  7.2 0.0 copy-start
  7.2 0.0 copy-start.2
  7.2 0.0 copy-start.3
  7.2 0.0 all-gather.5.cloned.1.call-start
  7.2 0.7 all-gather.5.cloned.1.call-update
  7.9 0.0 all-gather.7.cloned.1.call-start
  8.0 0.6 copy-done
  8.6 0.5 fusion.23
  9.1 5.8 all-reduce.1
  15.0 0.0 copy-done.2
  15.0 0.0 copy-done.3
  15.0 2.2 fusion.15
  17.1 2.0 collective-permute-start
  19.2 0.0 collective-permute-start.1
  19.2 0.0 all-gather.7.cloned.1.call-update
  19.2 0.0 all-gather.9.cloned.1.call-start
  19.3 33.6 %collective-permute-done.1 = f32[3072]{0:T(1024)S(1)} collective-permute-done((f32[3072]{0:T(1024)S(1)}, f32[3072]{0:T(1024)S(1)}, u32[]{:S(2)}, u32[]{:S(2)}) %collective-permute-start.1) | collective-permute-done | bytes 12320 | tf_op jit(solution)/shard_map/ppermute | solution.py:21
  52.9 0.0 collective-permute-done
  52.9 2.1 broadcast_select_fusion.1
  55.0 0.0 copy-start.4
  55.0 1.9 pad_maximum_fusion
  57.0 321.0 %all-gather.5.cloned.1.call-done = bf16[6144,6144]{1,0:T(8,128)(2,1)} async-done(((bf16[384,6144]{1,0:T(8,128)(2,1)}), bf16[6144,6144]{1,0:T(8,128)(2,1)}) %all-gather.5.cloned.1.call-update) | async-done | bytes 75497488 | tf_op jit(solution)/shard_map/all_gather | solution.py:94
  378.0 0.0 copy-done.4
  378.0 32.6 %fusion.13 = bf16[256,6144]{1,0:T(8,128)(2,1)} fusion(bf16[256,6144]{1,0:T(8,128)(2,1)} %pad_maximum_fusion, bf16[6144,6144]{1,0:T(8,128)(2,1)} %all-gather.5.cloned.1.call-done, bf16[256,6144]{1,0:T(8,128)(2,1)} %param.11, f32[6144]{0:T(1024)S(1)} %copy-done.4), kind=kOutput, calls=%fused_computation.15 | convolution fusion | flops 19346227200 | bytes 84959232 | tf_op jit(solution)/shard_map/dot_general | solution.py:112
  410.5 0.0 copy-start.5
  410.5 12.8 %fusion.2 = f32[256,1536]{1,0:T(8,128)S(1)} fusion(bf16[256,6144]{1,0:T(8,128)(2,1)} %fusion.13, bf16[6144,6144]{1,0:T(8,128)(2,1)} %all-gather.5.cloned.1.call-done), kind=kOutput, calls=%fused_computation.2 | convolution fusion | flops 4831838208 | bytes 23592960 | tf_op jit(solution)/shard_map/dot_general | solution.py:81
  423.3 0.0 copy-done.5
  423.3 10.0 %select_convert_fusion = (bf16[256,1536]{1,0:T(8,128)(2,1)}, f32[256,1536]{1,0:T(8,128)S(1)}) fusion(f32[256,1536]{1,0:T(8,128)S(1)} %fusion.2, pred[]{:T(512)S(6)} %eq.2, bf16[256,6144]{1,0:T(8,128)(2,1)S(1)} %copy-done.5, bf16[6144,6144]{1,0:T(8,128)(2,1)} %all-gather.5.cloned.1.call-done), kind=kOutput, calls=%fused_computation.45 | convolution fusion | flops 4832231424 | bytes 25952256 | tf_op jit(solution)/shard_map/dot_general | solution.py:81
  433.4 1.5 collective-permute-start.3
  434.8 9.2 %fusion.6 = f32[256,1536]{1,0:T(8,128)S(1)} fusion(bf16[256,6144]{1,0:T(8,128)(2,1)S(1)} %copy-done.5, bf16[6144,6144]{1,0:T(8,128)(2,1)} %all-gather.5.cloned.1.call-done), kind=kOutput, calls=%fused_computation.6 | convolution fusion | flops 4831838208 | bytes 23592960 | tf_op jit(solution)/shard_map/dot_general | solution.py:81
  444.1 0.0 copy-start.1
  444.1 11.3 %select_convert_fusion.1 = (bf16[256,1536]{1,0:T(8,128)(2,1)}, f32[256,1536]{1,0:T(8,128)}) fusion(f32[256,1536]{1,0:T(8,128)S(1)} %fusion.6, pred[]{:T(512)S(6)} %eq.2, bf16[256,6144]{1,0:T(8,128)(2,1)} %fusion.13, bf16[6144,6144]{1,0:T(8,128)(2,1)} %all-gather.5.cloned.1.call-done), kind=kOutput, calls=%fused_computation.47 | convolution fusion | flops 4832231424 | bytes 25952256 | tf_op jit(solution)/shard_map/dot_general | solution.py:81
  455.4 0.6 collective-permute-start.2
  456.0 0.0 collective-permute-done.3
  456.0 18.8 %collective-permute-done.2 = bf16[256,1536]{1,0:T(8,128)(2,1)S(1)} collective-permute-done((bf16[256,1536]{1,0:T(8,128)(2,1)}, bf16[256,1536]{1,0:T(8,128)(2,1)S(1)}, u32[]{:S(2)}, u32[]{:S(2)}) %collective-permute-start.2) | collective-permute-done | bytes 786464 | tf_op jit(solution)/shard_map/ppermute | solution.py:21
  474.8 0.0 copy-done.1
  474.8 4.1 multiply_reduce_fusion.2
  479.0 4.9 all-reduce
  483.9 4.3 fusion.22
  488.3 1.7 copy.10
  490.0 40.6 %all_to_all.5 = bf16[16,256,192]{1,2,0:T(8,128)(2,1)S(1)} all-to-all(bf16[16,256,192]{1,2,0:T(8,128)(2,1)S(1)} %bitcast.23), channel_id=1, replica_groups=mesh['dp'=16,'mp'=2] {'dp'}, dimensions={0} | all-to-all | bytes 3145728 | tf_op jit(solution)/shard_map/all_to_all | solution.py:61
  530.6 0.2 copy.12
  530.8 0.0 all-gather.7.cloned.1.call-done
  530.8 4.9 fusion.28
  535.8 0.0 all-gather.9.cloned.1.call-update
  535.8 48.4 %all-gather.9.cloned.1.call-done = bf16[3072,588]{1,0:T(8,128)(2,1)} async-done(((bf16[192,588]{1,0:T(8,128)(2,1)}), bf16[3072,588]{1,0:T(8,128)(2,1)}) %all-gather.9.cloned.1.call-update) | async-done | bytes 3612688 | tf_op jit(solution)/shard_map/all_gather | solution.py:63
  584.2 7.5 %spread_columns.1 = f32[588,3072]{1,0:T(8,128)} custom-call(bf16[16,192,588]{2,1,0:T(8,128)(2,1)} %bitcast.24), custom_call_target="tpu_custom_call" | custom-call | tf_op jit(solution)/shard_map/spread_columns/pallas_call | solution.py:40
  (7 shorter events, 0.0 us)
Async XLA Ops:
  7.2 1.4 copy-start
  7.2 7.8 %copy-start.2 = (bf16[256,3072]{1,0:T(8,128)(2,1)S(1)}, bf16[256,3072]{1,0:T(8,128)(2,1)}, u32[]{:S(2)}) copy-start(bf16[256,3072]{1,0:T(8,128)(2,1)} %param.10) | copy-start | bytes 4718596
  7.2 7.8 %copy-start.3 = (f32[3072]{0:T(1024)S(1)}, f32[3072]{0:T(1024)}, u32[]{:S(2)}) copy-start(f32[3072]{0:T(1024)} %param.14) | copy-start | bytes 36868
  7.2 370.8 %all-gather.5.cloned.1.call-start = ((), (), s32[]{:S(2)}) async-start(), calls=%async_computation.1 | async-start | bytes 80216064 | tf_op jit(solution)/shard_map/all_gather | solution.py:94
  7.9 522.9 %all-gather.7.cloned.1.call-start = ((), (), s32[]{:S(2)}) async-start(), calls=%async_computation.2 | async-start | bytes 5152768 | tf_op jit(solution)/shard_map/all_gather | solution.py:95
  17.1 35.8 %collective-permute-start = (bf16[256,3072]{1,0:T(8,128)(2,1)}, bf16[256,3072]{1,0:T(8,128)(2,1)}, u32[]{:S(2)}, u32[]{:S(2)}) collective-permute-start(bf16[256,3072]{1,0:T(8,128)(2,1)} %get-tuple-element.26), channel_id=1, source_target_pairs={{0,1},{1,0},{2,3},{3,2},{4,5},{5,4},{6,7},{7,6},{8,9},{9,8},{10,11... | collective-permute-start | bytes 4718600 | tf_op jit(solution)/shard_map/ppermute | solution.py:21
  19.2 33.7 %collective-permute-start.1 = (f32[3072]{0:T(1024)S(1)}, f32[3072]{0:T(1024)S(1)}, u32[]{:S(2)}, u32[]{:S(2)}) collective-permute-start(f32[3072]{0:T(1024)S(1)} %copy-done.3), channel_id=1, source_target_pairs={{0,1},{1,0},{2,3},{3,2},{4,5},{5,4},{6,7},{7,6},{8,9},{9,8},{10,11... | collective-permute-start | bytes 36872 | tf_op jit(solution)/shard_map/ppermute | solution.py:21
  19.2 564.9 %all-gather.9.cloned.1.call-start = ((), (), s32[]{:S(2)}) async-start(), calls=%async_computation.3 | async-start | bytes 4177920 | tf_op jit(solution)/shard_map/all_gather | solution.py:63
  55.0 322.9 %copy-start.4 = (f32[6144]{0:T(1024)S(1)}, f32[6144]{0:T(1024)}, u32[]{:S(2)}) copy-start(f32[6144]{0:T(1024)} %param.13) | copy-start | bytes 73732
  410.5 12.8 %copy-start.5 = (bf16[256,6144]{1,0:T(8,128)(2,1)S(1)}, bf16[256,6144]{1,0:T(8,128)(2,1)}, u32[]{:S(2)}) copy-start(bf16[256,6144]{1,0:T(8,128)(2,1)} %fusion.13) | copy-start | bytes 9437188
  433.4 22.7 %collective-permute-start.3 = (bf16[256,1536]{1,0:T(8,128)(2,1)}, bf16[256,1536]{1,0:T(8,128)(2,1)}, u32[]{:S(2)}, u32[]{:S(2)}) collective-permute-start(bf16[256,1536]{1,0:T(8,128)(2,1)} %get-tuple-element.35), channel_id=1, source_target_pairs={{0,1},{1,0},{2,3},{3,2},{4,5},{5,4},{6,7},{7,6},{8,9},{9,8},{10,11... | collective-permute-start | bytes 2359304 | tf_op jit(solution)/shard_map/ppermute | solution.py:21
  444.1 30.8 %copy-start.1 = (bf16[256,6144]{1,0:T(8,128)(2,1)S(1)}, bf16[256,6144]{1,0:T(8,128)(2,1)}, u32[]{:S(2)}) copy-start(bf16[256,6144]{1,0:T(8,128)(2,1)} %pad_maximum_fusion) | copy-start | bytes 9437188
  455.4 19.4 %collective-permute-start.2 = (bf16[256,1536]{1,0:T(8,128)(2,1)}, bf16[256,1536]{1,0:T(8,128)(2,1)S(1)}, u32[]{:S(2)}, u32[]{:S(2)}) collective-permute-start(bf16[256,1536]{1,0:T(8,128)(2,1)} %get-tuple-element.37), channel_id=1, source_target_pairs={{0,1},{1,0},{2,3},{3,2},{4,5},{5,4},{6,7},{7,6},{8,9},{9,8},{10,11... | collective-permute-start | bytes 2359304 | tf_op jit(solution)/shard_map/ppermute | solution.py:21
Sparse Core Ops, SparseCore 0:
  9.6 368.3 all-gather.4
  380.1 56.7 all-gather.6
  535.9 48.1 all-gather.8

commit v2 on v1

--- a/solution.py
+++ b/solution.py
@@ -8,7 +8,7 @@
 
 D = 6144
 IMAGES = 1
-PIECES = 2
+PIECES = 4
 
 
 def gelu_slope(values):
@@ -114,13 +114,15 @@
     own_sum, scaled_share, paired_share = branch_sum(delta, weight, normed, gain_all, groups)
     attn = attn_grad.astype(jnp.float32)
     attn_scaled = attn * norm_gain
-    scaled_total, paired_total = lax.psum(
-        (
+    shares = jnp.concatenate(
+        [
             scaled_share + jnp.sum(attn_scaled, axis=-1, keepdims=True),
             paired_share + jnp.sum(attn_scaled * unit, axis=-1, keepdims=True),
-        ),
-        "mp",
+        ],
+        axis=1,
     )
+    totals = shares + swap(shares) if groups == 2 else lax.psum(shares, "mp")
+    scaled_total, paired_total = totals[:, :1], totals[:, 1:]
     scaled = (own_sum + attn) * norm_gain
     norm_back = inv_std * (scaled - scaled_total / D - unit * (paired_total / D))
     embed_grad = (block_grad.astype(jnp.float32) + norm_back).astype(jnp.bfloat16)

time: 599 us -> 591 us (0.987)
  waiting for transfers between devices: 423 us -> 410 us
  matrix products: 80.9 us -> 90.1 us
    ppermute x4 -> x7, waiting for transfers between devices: 52.4 us -> 40.3 us  [swap(): return lax.ppermute(value, 'mp', [(0, 1), (1, 0)])]
    dot_general x4 -> x8, matrix products: 43.4 us -> 52.6 us  [branch_sum(): lax.dot_general(delta, weight[rows], transposed, preferred_element_type=j...]
  transfers between devices with their start and end apart: 7 -> 10, of which waited for: 4 -> 4; matrix products, arithmetic and copies ran while one was open for 16% -> 17% of each run, Pallas kernels for 0% -> 0%
where the time goes in v2:
time: 591 us; the launch traced here: 590 us
  waiting for transfers between devices  410 us (69%)
  matrix products  90.1 us (15%)
  blocking collectives  46.4 us (8%)
  between operations  14 us (2%)
  other arithmetic  11.3 us (2%)
  starting transfers between devices  8.05 us (1%)
  Pallas kernels  7.55 us (1%)
    all_gather x1, waiting for transfers between devices, body(): weight = lax.all_gather(up_weight, 'dp', axis=0, tiled=True)  321 us
    dot_general x8, matrix products, branch_sum(): lax.dot_general(delta, weight[rows], transposed, preferred_element_type=j...  52.6 us
    all_gather x1, waiting for transfers between devices, patch_grad(): lax.all_gather(part.astype(jnp.bfloat16), 'dp', axis=0)  48.4 us
    all_to_all x1, blocking collectives, patch_grad(): mine = lax.all_to_all(mine, 'dp', 0, 0)  40.6 us
    ppermute x7, waiting for transfers between devices, swap(): return lax.ppermute(value, 'mp', [(0, 1), (1, 0)])  40.3 us
    dot_general x1, matrix products, body(): jnp.dot(normed, weight, preferred_element_type=jnp.float32) + up_bias  32.5 us
  transfers between devices with their start and end apart: 10, of which 4 were waited for; matrix products, arithmetic and copies ran while one was open for 17% of the time, Pallas kernels for 0%

profile of v2, /device:TPU:0, one launch (start us, length us, event | category | flops | bytes accessed | tf_op | source)
XLA Modules:
  0.0 590.4 jit_solution(943932355215254913)
XLA Ops:
  7.2 0.0 copy-start
  7.2 0.0 copy-start.2
  7.2 0.0 copy-start.4
  7.2 0.0 all-gather.5.cloned.1.call-start
  7.2 0.7 all-gather.5.cloned.1.call-update
  7.9 0.0 all-gather.7.cloned.1.call-start
  8.0 0.6 copy-done
  8.6 0.5 fusion.31
  9.1 5.8 all-reduce
  15.0 0.0 copy-done.2
  15.0 0.0 copy-done.4
  15.0 2.1 fusion.23
  17.1 2.0 collective-permute-start
  19.2 0.0 collective-permute-start.1
  19.2 0.0 all-gather.7.cloned.1.call-update
  19.2 0.0 all-gather.9.cloned.1.call-start
  19.3 33.6 %collective-permute-done.1 = f32[3072]{0:T(1024)S(1)} collective-permute-done((f32[3072]{0:T(1024)S(1)}, f32[3072]{0:T(1024)S(1)}, u32[]{:S(2)}, u32[]{:S(2)}) %collective-permute-start.1) | collective-permute-done | bytes 12320 | tf_op jit(solution)/shard_map/ppermute | solution.py:21
  52.9 0.0 collective-permute-done
  52.9 2.1 broadcast_select_fusion.1
  55.0 0.0 copy-start.5
  55.0 1.9 pad_maximum_fusion
  56.9 321.0 %all-gather.5.cloned.1.call-done = bf16[6144,6144]{1,0:T(8,128)(2,1)} async-done(((bf16[384,6144]{1,0:T(8,128)(2,1)}), bf16[6144,6144]{1,0:T(8,128)(2,1)}) %all-gather.5.cloned.1.call-update) | async-done | bytes 75497488 | tf_op jit(solution)/shard_map/all_gather | solution.py:94
  378.0 0.0 copy-done.5
  378.0 32.5 %fusion.21 = bf16[256,6144]{1,0:T(8,128)(2,1)} fusion(bf16[256,6144]{1,0:T(8,128)(2,1)} %pad_maximum_fusion, bf16[6144,6144]{1,0:T(8,128)(2,1)} %all-gather.5.cloned.1.call-done, bf16[256,6144]{1,0:T(8,128)(2,1)} %param.11, f32[6144]{0:T(1024)S(1)} %copy-done.5), kind=kOutput, calls=%fused_computation.23 | convolution fusion | flops 19346227200 | bytes 84959232 | tf_op jit(solution)/shard_map/dot_general | solution.py:112
  410.5 0.0 copy-start.6
  410.5 7.5 %fusion.14 = f32[256,768]{1,0:T(8,128)S(1)} fusion(bf16[256,6144]{1,0:T(8,128)(2,1)} %fusion.21, bf16[6144,6144]{1,0:T(8,128)(2,1)} %all-gather.5.cloned.1.call-done), kind=kOutput, calls=%fused_computation.15 | convolution fusion | flops 2415919104 | bytes 13369344 | tf_op jit(solution)/shard_map/dot_general | solution.py:81
  418.0 0.0 copy-done.6
  418.0 6.4 %select_convert_fusion.3 = (bf16[256,768]{1,0:T(8,128)(2,1)S(1)}, f32[256,768]{1,0:T(8,128)S(1)}) fusion(f32[256,768]{1,0:T(8,128)S(1)} %fusion.14, pred[]{:T(512)S(6)} %eq.2, bf16[256,6144]{1,0:T(8,128)(2,1)S(1)} %copy-done.6, bf16[6144,6144]{1,0:T(8,128)(2,1)} %all-gather.5.cloned.1.call-done), kind=kOutput, calls=%fused_computation.71 | convolution fusion | flops 2416115712 | bytes 14548993 | tf_op jit(solution)/shard_map/dot_general | solution.py:81
  424.5 1.5 collective-permute-start.2
  426.0 6.4 %fusion.6 = f32[256,768]{1,0:T(8,128)S(1)} fusion(bf16[256,6144]{1,0:T(8,128)(2,1)S(1)} %copy-done.6, bf16[6144,6144]{1,0:T(8,128)(2,1)} %all-gather.5.cloned.1.call-done), kind=kOutput, calls=%fused_computation.7 | convolution fusion | flops 2415919104 | bytes 13369344 | tf_op jit(solution)/shard_map/dot_general | solution.py:81
  432.4 6.6 %select_convert_fusion.1 = (bf16[256,768]{1,0:T(8,128)(2,1)S(1)}, f32[256,768]{1,0:T(8,128)S(1)}) fusion(f32[256,768]{1,0:T(8,128)S(1)} %fusion.6, pred[]{:T(512)S(6)} %eq.2, bf16[256,6144]{1,0:T(8,128)(2,1)S(1)} %copy-done.6, bf16[6144,6144]{1,0:T(8,128)(2,1)} %all-gather.5.cloned.1.call-done), kind=kOutput, calls=%fused_computation.67 | convolution fusion | flops 2416115712 | bytes 14548993 | tf_op jit(solution)/shard_map/dot_general | solution.py:81
  439.0 0.4 collective-permute-start.4
  439.5 6.6 %fusion.2 = f32[256,768]{1,0:T(8,128)S(1)} fusion(bf16[256,6144]{1,0:T(8,128)(2,1)S(1)} %copy-done.6, bf16[6144,6144]{1,0:T(8,128)(2,1)} %all-gather.5.cloned.1.call-done), kind=kOutput, calls=%fused_computation.3 | convolution fusion | flops 2415919104 | bytes 13369344 | tf_op jit(solution)/shard_map/dot_general | solution.py:81
  446.0 6.3 %select_convert_fusion = (bf16[256,768]{1,0:T(8,128)(2,1)S(1)}, f32[256,768]{1,0:T(8,128)S(1)}) fusion(f32[256,768]{1,0:T(8,128)S(1)} %fusion.2, pred[]{:T(512)S(6)} %eq.2, bf16[256,6144]{1,0:T(8,128)(2,1)S(1)} %copy-done.6, bf16[6144,6144]{1,0:T(8,128)(2,1)} %all-gather.5.cloned.1.call-done), kind=kOutput, calls=%fused_computation.65 | convolution fusion | flops 2416115712 | bytes 14548993 | tf_op jit(solution)/shard_map/dot_general | solution.py:81
  452.3 1.7 collective-permute-start.5
  454.1 6.3 %fusion.10 = f32[256,768]{1,0:T(8,128)S(1)} fusion(bf16[256,6144]{1,0:T(8,128)(2,1)S(1)} %copy-done.6, bf16[6144,6144]{1,0:T(8,128)(2,1)} %all-gather.5.cloned.1.call-done), kind=kOutput, calls=%fused_computation.11 | convolution fusion | flops 2415919104 | bytes 13369344 | tf_op jit(solution)/shard_map/dot_general | solution.py:81
  460.4 0.0 copy-start.1
  460.4 6.5 %select_convert_fusion.2 = (bf16[256,768]{1,0:T(8,128)(2,1)S(1)}, f32[256,768]{1,0:T(8,128)S(1)}) fusion(f32[256,768]{1,0:T(8,128)S(1)} %fusion.10, pred[]{:T(512)S(6)} %eq.2, bf16[256,6144]{1,0:T(8,128)(2,1)S(1)} %copy-done.6, bf16[6144,6144]{1,0:T(8,128)(2,1)} %all-gather.5.cloned.1.call-done), kind=kOutput, calls=%fused_computation.69 | convolution fusion | flops 2416115712 | bytes 14548993 | tf_op jit(solution)/shard_map/dot_general | solution.py:81
  466.9 0.4 collective-permute-start.3
  467.3 0.0 copy-done.1
  467.3 0.9 multiply_reduce_fusion.6
  468.2 0.0 collective-permute-done.4
  468.2 0.3 multiply_reduce_fusion.11
  468.4 0.0 collective-permute-done.5
  468.5 0.3 multiply_reduce_fusion.9
  468.7 0.0 copy-start.3
  468.7 0.0 collective-permute-done.2
  468.7 0.2 multiply_reduce_fusion.14
  469.0 1.7 collective-permute-start.6
  470.7 6.7 %collective-permute-done.3 = bf16[256,768]{1,0:T(8,128)(2,1)S(1)} collective-permute-done((bf16[256,768]{1,0:T(8,128)(2,1)S(1)}, bf16[256,768]{1,0:T(8,128)(2,1)S(1)}, u32[]{:S(2)}, u32[]{:S(2)}) %collective-permute-start.3) | collective-permute-done | bytes 393248 | tf_op jit(solution)/shard_map/ppermute | solution.py:21
  477.4 0.1 convert_add_fusion.3
  477.5 0.0 collective-permute-done.6
  477.5 0.0 copy-done.3
  477.5 2.9 fusion.30
  480.4 1.7 copy.10
  482.1 40.6 %all_to_all.5 = bf16[16,256,192]{1,2,0:T(8,128)(2,1)S(1)} all-to-all(bf16[16,256,192]{1,2,0:T(8,128)(2,1)S(1)} %bitcast.27), channel_id=1, replica_groups=mesh['dp'=16,'mp'=2] {'dp'}, dimensions={0} | all-to-all | bytes 3145728 | tf_op jit(solution)/shard_map/all_to_all | solution.py:61
  522.7 0.2 copy.12
  522.9 0.0 all-gather.7.cloned.1.call-done
  522.9 4.9 fusion.36
  527.8 0.0 all-gather.9.cloned.1.call-update
  527.9 48.4 %all-gather.9.cloned.1.call-done = bf16[3072,588]{1,0:T(8,128)(2,1)} async-done(((bf16[192,588]{1,0:T(8,128)(2,1)}), bf16[3072,588]{1,0:T(8,128)(2,1)}) %all-gather.9.cloned.1.call-update) | async-done | bytes 3612688 | tf_op jit(solution)/shard_map/all_gather | solution.py:63
  576.3 7.5 %spread_columns.1 = f32[588,3072]{1,0:T(8,128)} custom-call(bf16[16,192,588]{2,1,0:T(8,128)(2,1)} %bitcast.28), custom_call_target="tpu_custom_call" | custom-call | tf_op jit(solution)/shard_map/spread_columns/pallas_call | solution.py:40
  (8 shorter events, 0.1 us)
Async XLA Ops:
  7.2 1.4 copy-start
  7.2 7.8 %copy-start.2 = (bf16[256,3072]{1,0:T(8,128)(2,1)S(1)}, bf16[256,3072]{1,0:T(8,128)(2,1)}, u32[]{:S(2)}) copy-start(bf16[256,3072]{1,0:T(8,128)(2,1)} %param.10) | copy-start | bytes 4718596
  7.2 7.8 %copy-start.4 = (f32[3072]{0:T(1024)S(1)}, f32[3072]{0:T(1024)}, u32[]{:S(2)}) copy-start(f32[3072]{0:T(1024)} %param.14) | copy-start | bytes 36868
  7.2 370.8 %all-gather.5.cloned.1.call-start = ((), (), s32[]{:S(2)}) async-start(), calls=%async_computation.1 | async-start | bytes 80216064 | tf_op jit(solution)/shard_map/all_gather | solution.py:94
  7.9 515.0 %all-gather.7.cloned.1.call-start = ((), (), s32[]{:S(2)}) async-start(), calls=%async_computation.2 | async-start | bytes 5152768 | tf_op jit(solution)/shard_map/all_gather | solution.py:95
  17.1 35.8 %collective-permute-start = (bf16[256,3072]{1,0:T(8,128)(2,1)}, bf16[256,3072]{1,0:T(8,128)(2,1)}, u32[]{:S(2)}, u32[]{:S(2)}) collective-permute-start(bf16[256,3072]{1,0:T(8,128)(2,1)} %get-tuple-element.25), channel_id=1, source_target_pairs={{0,1},{1,0},{2,3},{3,2},{4,5},{5,4},{6,7},{7,6},{8,9},{9,8},{10,11... | collective-permute-start | bytes 4718600 | tf_op jit(solution)/shard_map/ppermute | solution.py:21
  19.2 33.7 %collective-permute-start.1 = (f32[3072]{0:T(1024)S(1)}, f32[3072]{0:T(1024)S(1)}, u32[]{:S(2)}, u32[]{:S(2)}) collective-permute-start(f32[3072]{0:T(1024)S(1)} %copy-done.4), channel_id=1, source_target_pairs={{0,1},{1,0},{2,3},{3,2},{4,5},{5,4},{6,7},{7,6},{8,9},{9,8},{10,11... | collective-permute-start | bytes 36872 | tf_op jit(solution)/shard_map/ppermute | solution.py:21
  19.2 557.1 %all-gather.9.cloned.1.call-start = ((), (), s32[]{:S(2)}) async-start(), calls=%async_computation.3 | async-start | bytes 4177920 | tf_op jit(solution)/shard_map/all_gather | solution.py:63
  55.0 323.0 %copy-start.5 = (f32[6144]{0:T(1024)S(1)}, f32[6144]{0:T(1024)}, u32[]{:S(2)}) copy-start(f32[6144]{0:T(1024)} %param.13) | copy-start | bytes 73732
  410.5 7.5 %copy-start.6 = (bf16[256,6144]{1,0:T(8,128)(2,1)S(1)}, bf16[256,6144]{1,0:T(8,128)(2,1)}, u32[]{:S(2)}) copy-start(bf16[256,6144]{1,0:T(8,128)(2,1)} %fusion.21) | copy-start | bytes 9437188
  424.5 44.3 %collective-permute-start.2 = (bf16[256,768]{1,0:T(8,128)(2,1)S(1)}, bf16[256,768]{1,0:T(8,128)(2,1)S(1)}, u32[]{:S(2)}, u32[]{:S(2)}) collective-permute-start(bf16[256,768]{1,0:T(8,128)(2,1)S(1)} %get-tuple-element.54), channel_id=1, source_target_pairs={{0,1},{1,0},{2,3},{3,2},{4,5},{5,4},{6,7},{7,6},{8,9},{9,8},{10,11... | collective-permute-start | bytes 1179656 | tf_op jit(solution)/shard_map/ppermute | solution.py:21
  439.0 29.2 %collective-permute-start.4 = (bf16[256,768]{1,0:T(8,128)(2,1)S(1)}, bf16[256,768]{1,0:T(8,128)(2,1)S(1)}, u32[]{:S(2)}, u32[]{:S(2)}) collective-permute-start(bf16[256,768]{1,0:T(8,128)(2,1)S(1)} %get-tuple-element.50), channel_id=1, source_target_pairs={{0,1},{1,0},{2,3},{3,2},{4,5},{5,4},{6,7},{7,6},{8,9},{9,8},{10,11... | collective-permute-start | bytes 1179656 | tf_op jit(solution)/shard_map/ppermute | solution.py:21
  452.3 16.1 %collective-permute-start.5 = (bf16[256,768]{1,0:T(8,128)(2,1)S(1)}, bf16[256,768]{1,0:T(8,128)(2,1)S(1)}, u32[]{:S(2)}, u32[]{:S(2)}) collective-permute-start(bf16[256,768]{1,0:T(8,128)(2,1)S(1)} %get-tuple-element.48), channel_id=1, source_target_pairs={{0,1},{1,0},{2,3},{3,2},{4,5},{5,4},{6,7},{7,6},{8,9},{9,8},{10,11... | collective-permute-start | bytes 1179656 | tf_op jit(solution)/shard_map/ppermute | solution.py:21
  460.4 6.9 %copy-start.1 = (bf16[256,6144]{1,0:T(8,128)(2,1)S(1)}, bf16[256,6144]{1,0:T(8,128)(2,1)}, u32[]{:S(2)}) copy-start(bf16[256,6144]{1,0:T(8,128)(2,1)} %pad_maximum_fusion) | copy-start | bytes 9437188
  466.9 10.5 %collective-permute-start.3 = (bf16[256,768]{1,0:T(8,128)(2,1)S(1)}, bf16[256,768]{1,0:T(8,128)(2,1)S(1)}, u32[]{:S(2)}, u32[]{:S(2)}) collective-permute-start(bf16[256,768]{1,0:T(8,128)(2,1)S(1)} %get-tuple-element.52), channel_id=1, source_target_pairs={{0,1},{1,0},{2,3},{3,2},{4,5},{5,4},{6,7},{7,6},{8,9},{9,8},{10,11... | collective-permute-start | bytes 1179656 | tf_op jit(solution)/shard_map/ppermute | solution.py:21
  468.7 8.8 %copy-start.3 = (bf16[256,3072]{1,0:T(8,128)(2,1)S(1)}, bf16[256,3072]{1,0:T(8,128)(2,1)}, u32[]{:S(2)}) copy-start(bf16[256,3072]{1,0:T(8,128)(2,1)} %param.9) | copy-start | bytes 4718596
  469.0 8.5 %collective-permute-start.6 = (f32[256,2]{0,1:T(2,128)S(1)}, f32[256,2]{0,1:T(2,128)S(1)}, u32[]{:S(2)}, u32[]{:S(2)}) collective-permute-start(f32[256,2]{0,1:T(2,128)S(1)} %pad_maximum_fusion.2), channel_id=1, source_target_pairs={{0,1},{1,0},{2,3},{3,2},{4,5},{5,4},{6,7},{7,6},{8,9},{9,8},{10,11... | collective-permute-start | bytes 6152 | tf_op jit(solution)/shard_map/ppermute | solution.py:21
Sparse Core Ops, SparseCore 0:
  9.6 368.3 all-gather.4
  380.1 56.7 all-gather.6
  528.0 48.2 all-gather.8

commit v3 on v2

--- a/solution.py
+++ b/solution.py
@@ -8,7 +8,7 @@
 
 D = 6144
 IMAGES = 1
-PIECES = 4
+PIECES = 6
 
 
 def gelu_slope(values):

time: 591 us -> 600 us (1.015)
    dot_general x8 -> x12, matrix products: 52.6 us -> 57.4 us  [branch_sum(): lax.dot_general(delta, weight[rows], transposed, preferred_element_type=j...]
    ppermute x7 -> x9, waiting for transfers between devices: 40.3 us -> 41.7 us  [swap(): return lax.ppermute(value, 'mp', [(0, 1), (1, 0)])]
  transfers between devices with their start and end apart: 10 -> 12, of which waited for: 4 -> 5; matrix products, arithmetic and copies ran while one was open for 17% -> 17% of each run, Pallas kernels for 0% -> 0%
where the time goes in v3:
time: 600 us; the launch traced here: 599 us
  waiting for transfers between devices  412 us (69%)
  matrix products  94.9 us (16%)
  blocking collectives  46.8 us (8%)
  between operations  14 us (2%)
  other arithmetic  12.1 us (2%)
  starting transfers between devices  9.45 us (2%)
  Pallas kernels  7.55 us (1%)
    all_gather x1, waiting for transfers between devices, body(): weight = lax.all_gather(up_weight, 'dp', axis=0, tiled=True)  321 us
    dot_general x12, matrix products, branch_sum(): lax.dot_general(delta, weight[rows], transposed, preferred_element_type=j...  57.4 us
    all_gather x1, waiting for transfers between devices, patch_grad(): lax.all_gather(part.astype(jnp.bfloat16), 'dp', axis=0)  48.4 us
    ppermute x9, waiting for transfers between devices, swap(): return lax.ppermute(value, 'mp', [(0, 1), (1, 0)])  41.7 us
    all_to_all x1, blocking collectives, patch_grad(): mine = lax.all_to_all(mine, 'dp', 0, 0)  40.9 us
    dot_general x1, matrix products, body(): jnp.dot(normed, weight, preferred_element_type=jnp.float32) + up_bias  32.5 us
  transfers between devices with their start and end apart: 12, of which 5 were waited for; matrix products, arithmetic and copies ran while one was open for 17% of the time, Pallas kernels for 0%

profile of v3, /device:TPU:0, one launch (start us, length us, event | category | flops | bytes accessed | tf_op | source)
XLA Modules:
  0.0 599.2 jit_solution(15405457148540234643)
XLA Ops:
  7.2 0.0 all-gather.5.cloned.1.call-start
  7.2 0.7 all-gather.5.cloned.1.call-update
  7.9 0.0 all-gather.7.cloned.1.call-start
  8.0 0.6 copy-done
  8.6 0.5 fusion.39
  9.1 5.8 all-reduce
  15.0 2.1 fusion.31
  17.1 2.0 collective-permute-start
  19.2 0.0 collective-permute-start.1
  19.2 0.0 all-gather.7.cloned.1.call-update
  19.2 0.0 all-gather.9.cloned.1.call-start
  19.3 33.6 %collective-permute-done.1 = f32[3072]{0:T(1024)S(1)} collective-permute-done((f32[3072]{0:T(1024)S(1)}, f32[3072]{0:T(1024)S(1)}, u32[]{:S(2)}, u32[]{:S(2)}) %collective-permute-start.1) | collective-permute-done | bytes 12320 | tf_op jit(solution)/shard_map/ppermute | solution.py:21
  52.9 0.0 collective-permute-done
  52.9 2.1 broadcast_select_fusion.1
  55.0 0.0 copy-start.5
  55.0 1.9 pad_maximum_fusion
  56.9 321.0 %all-gather.5.cloned.1.call-done = bf16[6144,6144]{1,0:T(8,128)(2,1)} async-done(((bf16[384,6144]{1,0:T(8,128)(2,1)}), bf16[6144,6144]{1,0:T(8,128)(2,1)}) %all-gather.5.cloned.1.call-update) | async-done | bytes 75497488 | tf_op jit(solution)/shard_map/all_gather | solution.py:94
  378.0 0.0 copy-done.5
  378.0 32.5 %fusion.5 = bf16[256,6144]{1,0:T(8,128)(2,1)} fusion(bf16[256,6144]{1,0:T(8,128)(2,1)} %pad_maximum_fusion, bf16[6144,6144]{1,0:T(8,128)(2,1)} %all-gather.5.cloned.1.call-done, bf16[256,6144]{1,0:T(8,128)(2,1)} %param.11, f32[6144]{0:T(1024)S(1)} %copy-done.5), kind=kOutput, calls=%fused_computation.7 | convolution fusion | flops 19346227200 | bytes 84959232 | tf_op jit(solution)/shard_map/dot_general | solution.py:112
  410.5 5.8 fusion.28
  416.3 4.7 select_convert_fusion.5
  421.0 1.5 collective-permute-start.2
  422.5 4.7 fusion.24
  427.2 4.7 select_convert_fusion.4
  431.9 0.7 collective-permute-start.3
  432.6 4.7 fusion.20
  437.3 4.6 select_convert_fusion.3
  441.9 1.5 collective-permute-start.4
  443.4 4.9 fusion.16
  448.3 4.6 select_convert_fusion.2
  453.0 0.7 collective-permute-start.5
  453.6 4.7 fusion.12
  458.3 4.6 select_convert_fusion.1
  463.0 1.5 collective-permute-start.6
  464.4 4.7 fusion.8
  469.1 0.0 copy-start.1
  469.1 4.8 select_convert_fusion
  473.9 0.0 copy-done.1
  473.9 0.6 multiply_reduce_fusion.10
  474.5 0.0 collective-permute-done.2
  474.5 0.7 collective-permute-start.7
  475.2 0.2 multiply_reduce_fusion.22
  475.4 0.0 collective-permute-done.3
  475.4 0.4 multiply_reduce_fusion.11
  475.8 0.0 collective-permute-done.4
  475.9 0.2 multiply_reduce_fusion.18
  476.0 0.0 copy-start.3
  476.0 0.0 collective-permute-done.5
  476.0 0.2 multiply_reduce_fusion.17
  476.2 0.0 collective-permute-done.6
  476.3 0.2 multiply_reduce_fusion.15
  476.5 5.2 collective-permute-done.7
  481.6 0.5 multiply_reduce_fusion.13
  482.2 0.7 collective-permute-start.8
  482.9 2.9 collective-permute-done.8
  485.9 3.1 fusion.38
  488.9 1.7 copy.10
  490.6 40.9 %all_to_all.5 = bf16[16,256,192]{1,2,0:T(8,128)(2,1)S(1)} all-to-all(bf16[16,256,192]{1,2,0:T(8,128)(2,1)S(1)} %bitcast.31), channel_id=1, replica_groups=mesh['dp'=16,'mp'=2] {'dp'}, dimensions={0} | all-to-all | bytes 3145728 | tf_op jit(solution)/shard_map/all_to_all | solution.py:61
  531.6 0.2 copy.12
  531.8 0.0 all-gather.7.cloned.1.call-done
  531.8 4.9 fusion.44
  536.7 0.0 all-gather.9.cloned.1.call-update
  536.7 48.4 %all-gather.9.cloned.1.call-done = bf16[3072,588]{1,0:T(8,128)(2,1)} async-done(((bf16[192,588]{1,0:T(8,128)(2,1)}), bf16[3072,588]{1,0:T(8,128)(2,1)}) %all-gather.9.cloned.1.call-update) | async-done | bytes 3612688 | tf_op jit(solution)/shard_map/all_gather | solution.py:63
  585.1 7.5 %spread_columns.1 = f32[588,3072]{1,0:T(8,128)} custom-call(bf16[16,192,588]{2,1,0:T(8,128)(2,1)} %bitcast.32), custom_call_target="tpu_custom_call" | custom-call | tf_op jit(solution)/shard_map/spread_columns/pallas_call | solution.py:40
  (17 shorter events, 0.1 us)
Async XLA Ops:
  7.2 1.4 copy-start
  7.2 7.8 %copy-start.2 = (bf16[256,3072]{1,0:T(8,128)(2,1)S(1)}, bf16[256,3072]{1,0:T(8,128)(2,1)}, u32[]{:S(2)}) copy-start(bf16[256,3072]{1,0:T(8,128)(2,1)} %param.10) | copy-start | bytes 4718596
  7.2 7.8 %copy-start.4 = (f32[3072]{0:T(1024)S(1)}, f32[3072]{0:T(1024)}, u32[]{:S(2)}) copy-start(f32[3072]{0:T(1024)} %param.14) | copy-start | bytes 36868
  7.2 370.8 %all-gather.5.cloned.1.call-start = ((), (), s32[]{:S(2)}) async-start(), calls=%async_computation.1 | async-start | bytes 80216064 | tf_op jit(solution)/shard_map/all_gather | solution.py:94
  7.9 523.8 %all-gather.7.cloned.1.call-start = ((), (), s32[]{:S(2)}) async-start(), calls=%async_computation.2 | async-start | bytes 5152768 | tf_op jit(solution)/shard_map/all_gather | solution.py:95
  17.1 35.8 %collective-permute-start = (bf16[256,3072]{1,0:T(8,128)(2,1)}, bf16[256,3072]{1,0:T(8,128)(2,1)}, u32[]{:S(2)}, u32[]{:S(2)}) collective-permute-start(bf16[256,3072]{1,0:T(8,128)(2,1)} %get-tuple-element.30), channel_id=1, source_target_pairs={{0,1},{1,0},{2,3},{3,2},{4,5},{5,4},{6,7},{7,6},{8,9},{9,8},{10,11... | collective-permute-start | bytes 4718600 | tf_op jit(solution)/shard_map/ppermute | solution.py:21
  19.2 33.7 %collective-permute-start.1 = (f32[3072]{0:T(1024)S(1)}, f32[3072]{0:T(1024)S(1)}, u32[]{:S(2)}, u32[]{:S(2)}) collective-permute-start(f32[3072]{0:T(1024)S(1)} %copy-done.4), channel_id=1, source_target_pairs={{0,1},{1,0},{2,3},{3,2},{4,5},{5,4},{6,7},{7,6},{8,9},{9,8},{10,11... | collective-permute-start | bytes 36872 | tf_op jit(solution)/shard_map/ppermute | solution.py:21
  19.2 565.9 %all-gather.9.cloned.1.call-start = ((), (), s32[]{:S(2)}) async-start(), calls=%async_computation.3 | async-start | bytes 4177920 | tf_op jit(solution)/shard_map/all_gather | solution.py:63
  55.0 323.0 %copy-start.5 = (f32[6144]{0:T(1024)S(1)}, f32[6144]{0:T(1024)}, u32[]{:S(2)}) copy-start(f32[6144]{0:T(1024)} %param.13) | copy-start | bytes 73732
  410.5 5.8 copy-start.6
  421.0 53.5 %collective-permute-start.2 = (bf16[256,512]{1,0:T(8,128)(2,1)S(1)}, bf16[256,512]{1,0:T(8,128)(2,1)S(1)}, u32[]{:S(2)}, u32[]{:S(2)}) collective-permute-start(bf16[256,512]{1,0:T(8,128)(2,1)S(1)} %get-tuple-element.63), channel_id=1, source_target_pairs={{0,1},{1,0},{2,3},{3,2},{4,5},{5,4},{6,7},{7,6},{8,9},{9,8},{10,11... | collective-permute-start | bytes 786440 | tf_op jit(solution)/shard_map/ppermute | solution.py:21
  431.9 43.5 %collective-permute-start.3 = (bf16[256,512]{1,0:T(8,128)(2,1)S(1)}, bf16[256,512]{1,0:T(8,128)(2,1)S(1)}, u32[]{:S(2)}, u32[]{:S(2)}) collective-permute-start(bf16[256,512]{1,0:T(8,128)(2,1)S(1)} %get-tuple-element.65), channel_id=1, source_target_pairs={{0,1},{1,0},{2,3},{3,2},{4,5},{5,4},{6,7},{7,6},{8,9},{9,8},{10,11... | collective-permute-start | bytes 786440 | tf_op jit(solution)/shard_map/ppermute | solution.py:21
  441.9 33.9 %collective-permute-start.4 = (bf16[256,512]{1,0:T(8,128)(2,1)S(1)}, bf16[256,512]{1,0:T(8,128)(2,1)S(1)}, u32[]{:S(2)}, u32[]{:S(2)}) collective-permute-start(bf16[256,512]{1,0:T(8,128)(2,1)S(1)} %get-tuple-element.67), channel_id=1, source_target_pairs={{0,1},{1,0},{2,3},{3,2},{4,5},{5,4},{6,7},{7,6},{8,9},{9,8},{10,11... | collective-permute-start | bytes 786440 | tf_op jit(solution)/shard_map/ppermute | solution.py:21
  453.0 23.1 %collective-permute-start.5 = (bf16[256,512]{1,0:T(8,128)(2,1)S(1)}, bf16[256,512]{1,0:T(8,128)(2,1)S(1)}, u32[]{:S(2)}, u32[]{:S(2)}) collective-permute-start(bf16[256,512]{1,0:T(8,128)(2,1)S(1)} %get-tuple-element.69), channel_id=1, source_target_pairs={{0,1},{1,0},{2,3},{3,2},{4,5},{5,4},{6,7},{7,6},{8,9},{9,8},{10,11... | collective-permute-start | bytes 786440 | tf_op jit(solution)/shard_map/ppermute | solution.py:21
  463.0 13.3 %collective-permute-start.6 = (bf16[256,512]{1,0:T(8,128)(2,1)S(1)}, bf16[256,512]{1,0:T(8,128)(2,1)S(1)}, u32[]{:S(2)}, u32[]{:S(2)}) collective-permute-start(bf16[256,512]{1,0:T(8,128)(2,1)S(1)} %get-tuple-element.71), channel_id=1, source_target_pairs={{0,1},{1,0},{2,3},{3,2},{4,5},{5,4},{6,7},{7,6},{8,9},{9,8},{10,11... | collective-permute-start | bytes 786440 | tf_op jit(solution)/shard_map/ppermute | solution.py:21
  469.1 4.8 copy-start.1
  474.5 7.1 %collective-permute-start.7 = (bf16[256,512]{1,0:T(8,128)(2,1)S(1)}, bf16[256,512]{1,0:T(8,128)(2,1)S(1)}, u32[]{:S(2)}, u32[]{:S(2)}) collective-permute-start(bf16[256,512]{1,0:T(8,128)(2,1)S(1)} %get-tuple-element.73), channel_id=1, source_target_pairs={{0,1},{1,0},{2,3},{3,2},{4,5},{5,4},{6,7},{7,6},{8,9},{9,8},{10,11... | collective-permute-start | bytes 786440 | tf_op jit(solution)/shard_map/ppermute | solution.py:21
  476.0 9.8 %copy-start.3 = (bf16[256,3072]{1,0:T(8,128)(2,1)S(1)}, bf16[256,3072]{1,0:T(8,128)(2,1)}, u32[]{:S(2)}) copy-start(bf16[256,3072]{1,0:T(8,128)(2,1)} %param.9) | copy-start | bytes 4718596
  482.2 3.7 collective-permute-start.8
Sparse Core Ops, SparseCore 0:
  9.6 368.3 all-gather.4
  380.1 56.7 all-gather.6
  536.9 48.1 all-gather.8
